TPU v7x, 256 devices: a whole 4x4x8 slice. The times are simulated.
256 devices in a mesh: blk: 32 (over z, y_hi, core), grp: 8 (over y_lo, x).
Axes of the slice: x: 4, y: 4 (y_hi: 2, y_lo: 2; y = y_hi * 2 + y_lo), z: 8, core: 2. Of those that a mesh axis runs over, the one named last changes fastest.
Arguments:
- coeffs: bfloat16 [4096, 360, 128], P('blk', 'grp'), may hold values from -6 to 6
- vectors: float32 [4096, 16], P(('blk', 'grp')), may hold values from -6 to 6
Outputs:
- next_vectors: float32 [4096, 16], P(('blk', 'grp'))
All inputs are finite; a program needn't handle non-finite values.
Results may differ from a plain program's by a relative error of at most 0.0015.
The roundings to bfloat16 on the way count: a program that leaves them out, or rounds other values in their place, can miss the bound.
Values may be sent and summed in bfloat16 or wider, within the bound.
No kernel may reach another device: no remote copies, remote signals or barrier semaphores. Data moves between devices by JAX's collectives and lax.ppermute only.
A program may use at most 64 MiB of HBM per device.

v0:
```python
import math
import jax
import jax.numpy as jnp
from jax import lax
from jax.sharding import PartitionSpec as P

sharpness = 2.5
epsilon = 1e-06


def passed_along(block, axis, distance):
    devices = range(lax.axis_size(axis))
    route = [((i - distance) % len(devices), i) for i in devices]
    return lax.ppermute(block, axis, route)


def trig_rows(freq_local, group_size):
    total = freq_local * group_size
    row_ids = jnp.arange(2 * total, dtype=jnp.int32)
    within = row_ids % (2 * freq_local)
    freq = row_ids // (2 * freq_local) * freq_local + within % freq_local
    angles = jnp.arange(total, dtype=jnp.int32)
    phase = (freq[:, None] * angles[None, :] % total).astype(jnp.float32) * (2.0 * math.pi / total)
    cos_part = jnp.cos(phase).astype(jnp.bfloat16)
    sin_part = (-jnp.sin(phase)).astype(jnp.bfloat16)
    return jnp.where((within >= freq_local)[:, None], sin_part, cos_part)


def per_device(coeffs, vectors):
    block, freq_local, channels = coeffs.shape
    half_width = channels // 2
    group_size = lax.axis_size("grp")
    group_index = lax.axis_index("grp")
    own_rows = vectors.shape[0]
    angles = freq_local * group_size
    squares = jnp.einsum("ikc,ikc->i", coeffs, coeffs, preferred_element_type=jnp.float32)
    total_sq = lax.psum(squares, "grp")
    inv_norm = lax.rsqrt(total_sq / (angles * channels) + epsilon)
    unit_coef = (coeffs.astype(jnp.float32) * inv_norm[:, None, None]).astype(jnp.bfloat16)
    before_blk = passed_along(unit_coef, "blk", 1)
    after_blk = passed_along(unit_coef, "blk", -1)
    columns = jnp.concatenate([unit_coef, before_blk, after_blk], axis=0)
    swapped = jnp.concatenate([-columns[..., half_width:], columns[..., :half_width]], axis=-1)
    real_part = jnp.einsum("ikc,jkc->kij", unit_coef, columns, preferred_element_type=jnp.float32)
    imag_part = jnp.einsum("ikc,jkc->kij", unit_coef, swapped, preferred_element_type=jnp.float32)
    pair_terms = jnp.concatenate([real_part, imag_part], axis=0).astype(jnp.bfloat16)
    trig_table = trig_rows(freq_local, group_size)
    factor = sharpness / math.sqrt(angles * channels)
    corr = jnp.einsum(
        "frj,fm->rjm",
        lax.all_to_all(pair_terms, "grp", split_axis=1, concat_axis=0, tiled=True),
        trig_table,
        preferred_element_type=jnp.float32,
    )
    weights = jnp.mean(jnp.exp(factor * corr), axis=-1)
    col_ids = jnp.arange(weights.shape[1], dtype=jnp.int32)
    own_ids = group_index * own_rows + jnp.arange(own_rows, dtype=jnp.int32)
    weights = jnp.where(col_ids[None, :] == own_ids[:, None], jnp.zeros_like(weights), weights)
    row_degree = jnp.sum(weights, axis=-1)
    local_degree = jnp.sum(row_degree)
    degree_sum = lax.psum(local_degree, ("blk", "grp"))
    inv_root = lax.rsqrt(row_degree)
    scaled = vectors * inv_root[:, None]
    block_vec = lax.all_gather(scaled, "grp", axis=0, tiled=True)
    prev_vec = passed_along(block_vec, "blk", 1)
    next_vec = passed_along(block_vec, "blk", -1)
    neigh = jnp.concatenate([block_vec, prev_vec, next_vec], axis=0)
    product = jnp.dot(weights, neigh, precision=lax.Precision.HIGHEST)
    image = product * inv_root[:, None] * (3.0 * block)
    root_degree = jnp.sqrt(row_degree)
    local_proj = jnp.dot(root_degree, image, precision=lax.Precision.HIGHEST)
    projection = lax.psum(local_proj, ("blk", "grp"))
    deflated = image - root_degree[:, None] * (projection / degree_sum)[None, :]
    column_sq = lax.psum(jnp.sum(deflated * deflated, axis=0), ("blk", "grp"))
    total_rows = own_rows * group_size * lax.axis_size("blk")
    return deflated * lax.rsqrt(column_sq / total_rows + epsilon)[None, :]


def solution(mesh):
    placed = (P("blk", "grp", None), P(("blk", "grp"), None))
    return jax.shard_map(
        per_device, mesh=mesh, in_specs=placed, out_specs=P(("blk", "grp"), None), check_vma=False
    )
```

profile of v0, /device:TPU:1, one launch (start us, length us, event | category | flops | bytes accessed | tf_op | source)
XLA Modules:
  0.0 412.6 jit_solution(10428899602804066392)
XLA Ops:
  0.0 1.8 fusion.8
  1.8 16.8 %psum.28 = f32[128]{0:T(128)S(1)} all-reduce(f32[128]{0:T(128)S(1)} %fusion.8), channel_id=1, replica_groups=mesh['blk'=32,'grp'=8] {'grp'}, use_global_device_ids=true, to_apply=%region_0.0 | all-reduce | flops 128 | bytes 1024 | tf_op jit(solution)/shard_map/psum | solution.py:37
  18.5 1.9 multiply_convert_fusion
  20.4 7.0 %collective-permute-start = (bf16[128,45,128]{2,0,1:T(8,128)(2,1)S(1)}, bf16[128,45,128]{2,0,1:T(8,128)(2,1)S(1)}, u32[]{:S(2)}, u32[]{:S(2)}) collective-permute-start(bf16[128,45,128]{2,0,1:T(8,128)(2,1)S(1)} %multiply_convert_fusion), channel_id=1, source_target_pairs={{248,0},{0,8},{8,16},{16,24},{24,32},{32,40},{40,48},{48,56},{56,6... | collective-permute-start | bytes 4423688 | tf_op jit(solution)/shard_map/ppermute | solution.py:14
  27.5 32.1 %collective-permute-done = bf16[128,45,128]{2,0,1:T(8,128)(2,1)S(1)} collective-permute-done((bf16[128,45,128]{2,0,1:T(8,128)(2,1)S(1)}, bf16[128,45,128]{2,0,1:T(8,128)(2,1)S(1)}, u32[]{:S(2)}, u32[]{:S(2)}) %collective-permute-start) | collective-permute-done | bytes 1474592 | tf_op jit(solution)/shard_map/ppermute | solution.py:14
  59.6 2.9 collective-permute-done.1
  62.5 1.1 copy-done
  64.3 3.2 slice_negate_fusion
  67.5 7.4 %fusion.9 = bf16[45,128,384]{2,1,0:T(8,128)(2,1)} fusion(bf16[128,45,128]{2,0,1:T(8,128)(2,1)S(1)} %multiply_convert_fusion, bf16[384,45,64]{2,0,1:T(8,128)(2,1)} %get-tuple-element.10, bf16[384,45,64]{2,0,1:T(8,128)(2,1)S(1)} %get-tuple-element.9), kind=kOutput, calls=%fused_computation.13 | convolution fusion | flops 577290240 | bytes 10321920 | tf_op jit(solution)/shard_map/ikc,jkc->kij/dot_general | solution.py:45
  74.9 3.8 convolution_convert_fusion
  78.7 8.0 %pad_maximum_fusion = bf16[90,128,384]{2,1,0:T(8,128)(2,1)} fusion(bf16[45,128,384]{2,1,0:T(8,128)(2,1)} %fusion.9, bf16[45,128,384]{2,1,0:T(8,128)(2,1)} %convolution_convert_fusion), kind=kLoop, calls=%fused_computation | loop fusion | flops 4423680 | bytes 17694720 | tf_op jit(solution)/shard_map/concatenate | solution.py:46
  86.7 12.5 %copy.18 = bf16[90,128,384]{2,0,1:T(8,128)(2,1)} copy(bf16[90,128,384]{2,1,0:T(8,128)(2,1)} %pad_maximum_fusion) | data formatting | bytes 17694720 | tf_op jit(solution)/shard_map/concatenate | solution.py:46
  99.2 5.3 %all-to-all-start = ((bf16[90,128,384]{2,0,1:T(8,128)(2,1)}), bf16[90,128,384]{2,0,1:T(8,128)(2,1)}, u32[]{:S(2)}, u32[]{:S(2)}) async-start(bf16[90,128,384]{2,0,1:T(8,128)(2,1)} %copy.18), calls=%async_computation | async-start | bytes 18874368 | tf_op jit(solution)/shard_map/all_to_all | solution.py:51
  104.5 91.0 %all-to-all-done = bf16[90,128,384]{2,0,1:T(8,128)(2,1)} async-done(((bf16[90,128,384]{2,0,1:T(8,128)(2,1)}), bf16[90,128,384]{2,0,1:T(8,128)(2,1)}, u32[]{:S(2)}, u32[]{:S(2)}) %all-to-all-start) | async-done | bytes 8847392 | tf_op jit(solution)/shard_map/all_to_all | solution.py:51
  195.6 10.7 %copy.20 = bf16[8,90,16,384]{3,2,1,0:T(8,128)(2,1)} copy(bf16[8,90,16,384]{3,1,2,0:T(8,128)(2,1)} %bitcast.4) | data formatting | bytes 17694720 | tf_op jit(solution)/shard_map/all_to_all | solution.py:51
  206.2 12.9 %exponential_reduce_fusion = f32[16,384]{1,0:T(8,128)S(1)} fusion(bf16[720,16,384]{2,1,0:T(8,128)(2,1)} %bitcast.18, s32[720]{0:T(1024)S(1)} %fusion.39, pred[720]{0:T(1024)(128)(4,1)S(1)} %fusion.44), kind=kOutput, calls=%fused_computation.3 | convolution fusion | flops 3192836608 | bytes 8875536 | tf_op jit(solution)/shard_map/frj,fm->rjm/dot_general | solution.py:49
  219.1 0.7 fusion.32
  219.9 21.8 %all_gather.3 = f32[128,16]{1,0:T(8,128)S(1)} all-gather(f32[16,16]{1,0:T(8,128)S(1)} %broadcast_multiply_fusion), channel_id=1, replica_groups=mesh['blk'=32,'grp'=8] {'grp'}, dimensions={0}, use_global_device_ids=true | all-gather | bytes 9216 | tf_op jit(solution)/shard_map/all_gather | solution.py:64
  241.7 9.5 %collective-permute-start.2 = (f32[128,16]{1,0:T(8,128)S(1)}, f32[128,16]{1,0:T(8,128)S(1)}, u32[]{:S(2)}, u32[]{:S(2)}) collective-permute-start(f32[128,16]{1,0:T(8,128)S(1)} %all_gather.3), channel_id=1, source_target_pairs={{248,0},{0,8},{8,16},{16,24},{24,32},{32,40},{40,48},{48,56},{56,6... | collective-permute-start | bytes 24584 | tf_op jit(solution)/shard_map/ppermute | solution.py:14
  251.2 1.3 collective-permute-done.2
  252.5 3.8 collective-permute-done.3
  256.8 81.0 %all-reduce = (f32[16]{0:T(128)S(1)}, f32[]{:T(128)}) all-reduce(f32[16]{0:T(128)S(1)} %convolution_bitcast_fusion, f32[]{:T(128)} %get-tuple-element.5), channel_id=1, replica_groups=mesh['blk'=32,'grp'=8] {'blk','grp'}, use_global_device_ids=true, to_apply=%region_3.4 | all-reduce | flops 17 | bytes 136 | tf_op jit(solution)/shard_map/psum | solution.py:72
  338.6 73.4 %psum.31 = f32[16]{0:T(128)S(1)} all-reduce(f32[16]{0:T(128)S(1)} %multiply_reduce_fusion), channel_id=1, replica_groups=mesh['blk'=32,'grp'=8] {'blk','grp'}, use_global_device_ids=true, to_apply=%region_7.8 | all-reduce | flops 16 | bytes 128 | tf_op jit(solution)/shard_map/psum | solution.py:74
  412.0 0.7 fusion.37
  (22 shorter events, 2.1 us)
Async XLA Ops:
  20.4 39.1 %collective-permute-start = (bf16[128,45,128]{2,0,1:T(8,128)(2,1)S(1)}, bf16[128,45,128]{2,0,1:T(8,128)(2,1)S(1)}, u32[]{:S(2)}, u32[]{:S(2)}) collective-permute-start(bf16[128,45,128]{2,0,1:T(8,128)(2,1)S(1)} %multiply_convert_fusion), channel_id=1, source_target_pairs={{248,0},{0,8},{8,16},{16,24},{24,32},{32,40},{40,48},{48,56},{56,6... | collective-permute-start | bytes 4423688 | tf_op jit(solution)/shard_map/ppermute | solution.py:14
  27.5 35.0 %collective-permute-start.1 = (bf16[128,45,128]{2,0,1:T(8,128)(2,1)S(1)}, bf16[128,45,128]{2,0,1:T(8,128)(2,1)S(1)}, u32[]{:S(2)}, u32[]{:S(2)}) collective-permute-start(bf16[128,45,128]{2,0,1:T(8,128)(2,1)S(1)} %multiply_convert_fusion), channel_id=1, source_target_pairs={{8,0},{16,8},{24,16},{32,24},{40,32},{48,40},{56,48},{64,56},{72,6... | collective-permute-start | bytes 4423688 | tf_op jit(solution)/shard_map/ppermute | solution.py:14
  62.5 1.1 copy-start
  67.5 7.4 %copy-start.1 = (bf16[128,45,128]{2,0,1:T(8,128)(2,1)S(1)}, bf16[128,45,128]{2,0,1:T(8,128)(2,1)}, u32[]{:S(2)}) copy-start(bf16[128,45,128]{2,0,1:T(8,128)(2,1)} %copy-done) | copy-start | bytes 4423684
  99.2 96.4 %all-to-all-start = ((bf16[90,128,384]{2,0,1:T(8,128)(2,1)}), bf16[90,128,384]{2,0,1:T(8,128)(2,1)}, u32[]{:S(2)}, u32[]{:S(2)}) async-start(bf16[90,128,384]{2,0,1:T(8,128)(2,1)} %copy.18), calls=%async_computation | async-start | bytes 18874368 | tf_op jit(solution)/shard_map/all_to_all | solution.py:51
  206.2 13.6 %copy-start.2 = (f32[16,16]{1,0:T(8,128)S(1)}, f32[16,16]{1,0:T(8,128)}, u32[]{:S(2)}) copy-start(f32[16,16]{1,0:T(8,128)} %param.3) | copy-start | bytes 3076
  241.7 10.8 %collective-permute-start.2 = (f32[128,16]{1,0:T(8,128)S(1)}, f32[128,16]{1,0:T(8,128)S(1)}, u32[]{:S(2)}, u32[]{:S(2)}) collective-permute-start(f32[128,16]{1,0:T(8,128)S(1)} %all_gather.3), channel_id=1, source_target_pairs={{248,0},{0,8},{8,16},{16,24},{24,32},{32,40},{40,48},{48,56},{56,6... | collective-permute-start | bytes 24584 | tf_op jit(solution)/shard_map/ppermute | solution.py:14
  251.1 5.2 %collective-permute-start.3 = (f32[128,16]{1,0:T(8,128)S(1)}, f32[128,16]{1,0:T(8,128)S(1)}, u32[]{:S(2)}, u32[]{:S(2)}) collective-permute-start(f32[128,16]{1,0:T(8,128)S(1)} %all_gather.3), channel_id=1, source_target_pairs={{8,0},{16,8},{24,16},{32,24},{40,32},{48,40},{56,48},{64,56},{72,6... | collective-permute-start | bytes 24584 | tf_op jit(solution)/shard_map/ppermute | solution.py:14
where the time goes:
time: 413 us
  blocking collectives  193 us (47%)
  waiting for transfers between devices  131 us (32%)
  matrix products  24.5 us (6%)
  local copies, waits for them, and re-layouts  24.4 us (6%)
  starting transfers between devices  21.8 us (5%)
  other arithmetic  17.7 us (4%)
    all_to_all x1, waiting for transfers between devices, per_device(): lax.all_to_all(pair_terms, 'grp', split_axis=1, concat_axis=0, tiled=True)  91 us
    psum x1, blocking collectives, per_device(): projection = lax.psum(local_proj, ('blk', 'grp'))  81 us
    psum x1, blocking collectives, per_device(): column_sq = lax.psum(jnp.sum(deflated * deflated, axis=0), ('blk', 'grp'))  73.4 us
    ppermute x4, waiting for transfers between devices, passed_along(): return lax.ppermute(block, axis, route)  40.1 us
    all_gather x1, blocking collectives, per_device(): block_vec = lax.all_gather(scaled, 'grp', axis=0, tiled=True)  21.8 us
    psum x1, blocking collectives, per_device(): total_sq = lax.psum(squares, 'grp')  16.8 us
    ppermute x4, starting transfers between devices, passed_along(): return lax.ppermute(block, axis, route)  16.5 us
    dot_general x1, matrix products, per_device(): jnp.einsum('frj,fm->rjm', lax.all_to_all(pair_terms, 'grp', split_axis=1,...  12.9 us
  transfers between devices with their start and end apart: 5, of which 5 were waited for; matrix products, arithmetic and copies ran while one was open for 0% of the time, Pallas kernels for 0%

commit v1 on v0

--- a/solution.py
+++ b/solution.py
@@ -48,7 +48,12 @@
     factor = sharpness / math.sqrt(angles * channels)
     corr = jnp.einsum(
         "frj,fm->rjm",
-        lax.all_to_all(pair_terms, "grp", split_axis=1, concat_axis=0, tiled=True),
+        jnp.concatenate(
+            lax.all_to_all(
+                jnp.stack(jnp.split(pair_terms, lax.axis_size("grp"), axis=1)), "grp", 0, 0
+            ),
+            axis=0,
+        ),
         trig_table,
         preferred_element_type=jnp.float32,
     )

time: 413 us -> 378 us (0.915)
  local copies, waits for them, and re-layouts: 24.4 us -> 1.3 us
  waiting for transfers between devices: 131 us -> 125 us
    concatenate x1 -> x0, local copies, waits for them, and re-layouts: 12.5 us -> none  [per_device(): jnp.concatenate([real_part, imag_part], axis=0).astype(jnp.bfloat16)]
    all_to_all x1 -> x0, local copies, waits for them, and re-layouts: 10.7 us -> none  [per_device(): lax.all_to_all(pair_terms, 'grp', split_axis=1, concat_axis=0, tiled=True)]
    unnamed x0 -> x7, other arithmetic: none -> 8.12 us
    concatenate x1 -> x0, other arithmetic: 8.01 us -> none  [per_device(): jnp.concatenate([real_part, imag_part], axis=0).astype(jnp.bfloat16)]
    all_to_all x1, waiting for transfers between devices: 91 us -> 84.8 us  [per_device(): lax.all_to_all(jnp.stack(jnp.split(pair_terms, lax.axis_size('grp'), axis...]
where the time goes in v1:
time: 378 us
  blocking collectives  190 us (50%)
  waiting for transfers between devices  125 us (33%)
  starting transfers between devices  21.7 us (6%)
  matrix products  20.9 us (6%)
  other arithmetic  19 us (5%)
    all_to_all x1, waiting for transfers between devices, per_device(): lax.all_to_all(jnp.stack(jnp.split(pair_terms, lax.axis_size('grp'), axis...  84.8 us
    psum x1, blocking collectives, per_device(): projection = lax.psum(local_proj, ('blk', 'grp'))  78.1 us
    psum x1, blocking collectives, per_device(): column_sq = lax.psum(jnp.sum(deflated * deflated, axis=0), ('blk', 'grp'))  73.4 us
    ppermute x4, waiting for transfers between devices, passed_along(): return lax.ppermute(block, axis, route)  40.1 us
    all_gather x1, blocking collectives, per_device(): block_vec = lax.all_gather(scaled, 'grp', axis=0, tiled=True)  21.8 us
    psum x1, blocking collectives, per_device(): total_sq = lax.psum(squares, 'grp')  16.8 us
    ppermute x4, starting transfers between devices, passed_along(): return lax.ppermute(block, axis, route)  16.5 us
    dot_general x1, matrix products, per_device(): jnp.einsum('frj,fm->rjm', jnp.concatenate(lax.all_to_all(jnp.stack(jnp.sp...  12.6 us
  transfers between devices with their start and end apart: 5, of which 5 were waited for; matrix products, arithmetic and copies ran while one was open for 0% of the time, Pallas kernels for 0%

profile of v1, /device:TPU:1, one launch (start us, length us, event | category | flops | bytes accessed | tf_op | source)
XLA Modules:
  0.0 377.9 jit_solution(5380752929334837688)
XLA Ops:
  0.0 1.8 fusion.8
  1.8 16.8 %psum.28 = f32[128]{0:T(128)S(1)} all-reduce(f32[128]{0:T(128)S(1)} %fusion.8), channel_id=1, replica_groups=mesh['blk'=32,'grp'=8] {'grp'}, use_global_device_ids=true, to_apply=%region_0.0 | all-reduce | flops 128 | bytes 1024 | tf_op jit(solution)/shard_map/psum | solution.py:37
  18.5 1.9 multiply_convert_fusion
  20.4 7.0 %collective-permute-start = (bf16[128,45,128]{2,0,1:T(8,128)(2,1)S(1)}, bf16[128,45,128]{2,0,1:T(8,128)(2,1)S(1)}, u32[]{:S(2)}, u32[]{:S(2)}) collective-permute-start(bf16[128,45,128]{2,0,1:T(8,128)(2,1)S(1)} %multiply_convert_fusion), channel_id=1, source_target_pairs={{248,0},{0,8},{8,16},{16,24},{24,32},{32,40},{40,48},{48,56},{56,6... | collective-permute-start | bytes 4423688 | tf_op jit(solution)/shard_map/ppermute | solution.py:14
  27.5 32.1 %collective-permute-done = bf16[128,45,128]{2,0,1:T(8,128)(2,1)S(1)} collective-permute-done((bf16[128,45,128]{2,0,1:T(8,128)(2,1)S(1)}, bf16[128,45,128]{2,0,1:T(8,128)(2,1)S(1)}, u32[]{:S(2)}, u32[]{:S(2)}) %collective-permute-start) | collective-permute-done | bytes 1474592 | tf_op jit(solution)/shard_map/ppermute | solution.py:14
  59.6 2.9 collective-permute-done.1
  64.3 3.2 slice_negate_fusion
  67.5 5.3 %fusion.9 = bf16[45,128,384]{2,1,0:T(8,128)(2,1)S(1)} fusion(bf16[128,45,128]{2,0,1:T(8,128)(2,1)S(1)} %multiply_convert_fusion, bf16[384,45,64]{2,0,1:T(8,128)(2,1)} %get-tuple-element.10, bf16[384,45,64]{2,0,1:T(8,128)(2,1)S(1)} %get-tuple-element.9), kind=kOutput, calls=%fused_computation.26 | convolution fusion | flops 577290240 | bytes 10321920 | tf_op jit(solution)/shard_map/ikc,jkc->kij/dot_general | solution.py:45
  72.8 2.5 convolution_convert_fusion
  75.4 1.2 bitcast_dynamic-update-slice_fusion.6
  76.6 1.2 bitcast_dynamic-update-slice_fusion.5
  78.9 1.2 bitcast_dynamic-update-slice_fusion.3
  80.1 1.1 bitcast_dynamic-update-slice_fusion.2
  82.3 1.2 bitcast_dynamic-update-slice_fusion
  83.5 1.2 fusion.23
  84.7 5.2 %all-to-all-start = ((bf16[8,90,16,384]{3,2,1,0:T(8,128)(2,1)}), bf16[8,90,16,384]{3,2,1,0:T(8,128)(2,1)}, u32[]{:S(2)}, u32[]{:S(2)}) async-start(bf16[8,90,16,384]{3,2,1,0:T(8,128)(2,1)} %fusion.23), calls=%async_computation | async-start | bytes 17694720 | tf_op jit(solution)/shard_map/all_to_all | solution.py:52
  89.9 84.8 %all-to-all-done = bf16[8,90,16,384]{3,2,1,0:T(8,128)(2,1)} async-done(((bf16[8,90,16,384]{3,2,1,0:T(8,128)(2,1)}), bf16[8,90,16,384]{3,2,1,0:T(8,128)(2,1)}, u32[]{:S(2)}, u32[]{:S(2)}) %all-to-all-start) | async-done | bytes 8847392 | tf_op jit(solution)/shard_map/all_to_all | solution.py:52
  174.7 12.6 %exponential_reduce_fusion = f32[16,384]{1,0:T(8,128)S(1)} fusion(bf16[720,16,384]{2,1,0:T(8,128)(2,1)} %bitcast.10, s32[720]{0:T(1024)S(1)} %fusion.48, pred[720]{0:T(1024)(128)(4,1)S(1)} %fusion.53), kind=kOutput, calls=%fused_computation.16 | convolution fusion | flops 3192836608 | bytes 8875536 | tf_op jit(solution)/shard_map/frj,fm->rjm/dot_general | solution.py:49
  188.0 21.8 %all_gather.3 = f32[128,16]{1,0:T(8,128)S(1)} all-gather(f32[16,16]{1,0:T(8,128)S(1)} %broadcast_multiply_fusion), channel_id=1, replica_groups=mesh['blk'=32,'grp'=8] {'grp'}, dimensions={0}, use_global_device_ids=true | all-gather | bytes 9216 | tf_op jit(solution)/shard_map/all_gather | solution.py:69
  209.8 9.5 %collective-permute-start.2 = (f32[128,16]{1,0:T(8,128)S(1)}, f32[128,16]{1,0:T(8,128)S(1)}, u32[]{:S(2)}, u32[]{:S(2)}) collective-permute-start(f32[128,16]{1,0:T(8,128)S(1)} %all_gather.3), channel_id=1, source_target_pairs={{248,0},{0,8},{8,16},{16,24},{24,32},{32,40},{40,48},{48,56},{56,6... | collective-permute-start | bytes 24584 | tf_op jit(solution)/shard_map/ppermute | solution.py:14
  219.4 1.3 collective-permute-done.2
  220.7 3.8 %collective-permute-done.3 = f32[128,16]{1,0:T(8,128)S(1)} collective-permute-done((f32[128,16]{1,0:T(8,128)S(1)}, f32[128,16]{1,0:T(8,128)S(1)}, u32[]{:S(2)}, u32[]{:S(2)}) %collective-permute-start.3) | collective-permute-done | bytes 8224 | tf_op jit(solution)/shard_map/ppermute | solution.py:14
  224.9 78.1 %all-reduce = (f32[16]{0:T(128)S(1)}, f32[]{:T(128)}) all-reduce(f32[16]{0:T(128)S(1)} %convolution_bitcast_fusion, f32[]{:T(128)} %get-tuple-element.5), channel_id=1, replica_groups=mesh['blk'=32,'grp'=8] {'blk','grp'}, use_global_device_ids=true, to_apply=%region_3.4 | all-reduce | flops 17 | bytes 136 | tf_op jit(solution)/shard_map/psum | solution.py:77
  303.8 73.4 %psum.31 = f32[16]{0:T(128)S(1)} all-reduce(f32[16]{0:T(128)S(1)} %multiply_reduce_fusion), channel_id=1, replica_groups=mesh['blk'=32,'grp'=8] {'blk','grp'}, use_global_device_ids=true, to_apply=%region_7.8 | all-reduce | flops 16 | bytes 128 | tf_op jit(solution)/shard_map/psum | solution.py:79
  (27 shorter events, 6.8 us)
Async XLA Ops:
  20.4 39.1 %collective-permute-start = (bf16[128,45,128]{2,0,1:T(8,128)(2,1)S(1)}, bf16[128,45,128]{2,0,1:T(8,128)(2,1)S(1)}, u32[]{:S(2)}, u32[]{:S(2)}) collective-permute-start(bf16[128,45,128]{2,0,1:T(8,128)(2,1)S(1)} %multiply_convert_fusion), channel_id=1, source_target_pairs={{248,0},{0,8},{8,16},{16,24},{24,32},{32,40},{40,48},{48,56},{56,6... | collective-permute-start | bytes 4423688 | tf_op jit(solution)/shard_map/ppermute | solution.py:14
  27.5 35.0 %collective-permute-start.1 = (bf16[128,45,128]{2,0,1:T(8,128)(2,1)S(1)}, bf16[128,45,128]{2,0,1:T(8,128)(2,1)S(1)}, u32[]{:S(2)}, u32[]{:S(2)}) collective-permute-start(bf16[128,45,128]{2,0,1:T(8,128)(2,1)S(1)} %multiply_convert_fusion), channel_id=1, source_target_pairs={{8,0},{16,8},{24,16},{32,24},{40,32},{48,40},{56,48},{64,56},{72,6... | collective-permute-start | bytes 4423688 | tf_op jit(solution)/shard_map/ppermute | solution.py:14
  62.5 1.1 copy-start
  67.5 5.3 %copy-start.1 = (bf16[128,45,128]{2,0,1:T(8,128)(2,1)S(1)}, bf16[128,45,128]{2,0,1:T(8,128)(2,1)}, u32[]{:S(2)}) copy-start(bf16[128,45,128]{2,0,1:T(8,128)(2,1)} %copy-done) | copy-start | bytes 4423684
  84.7 90.0 %all-to-all-start = ((bf16[8,90,16,384]{3,2,1,0:T(8,128)(2,1)}), bf16[8,90,16,384]{3,2,1,0:T(8,128)(2,1)}, u32[]{:S(2)}, u32[]{:S(2)}) async-start(bf16[8,90,16,384]{3,2,1,0:T(8,128)(2,1)} %fusion.23), calls=%async_computation | async-start | bytes 17694720 | tf_op jit(solution)/shard_map/all_to_all | solution.py:52
  174.6 13.3 %copy-start.2 = (f32[16,16]{1,0:T(8,128)S(1)}, f32[16,16]{1,0:T(8,128)}, u32[]{:S(2)}) copy-start(f32[16,16]{1,0:T(8,128)} %param.3) | copy-start | bytes 3076
  209.8 10.8 %collective-permute-start.2 = (f32[128,16]{1,0:T(8,128)S(1)}, f32[128,16]{1,0:T(8,128)S(1)}, u32[]{:S(2)}, u32[]{:S(2)}) collective-permute-start(f32[128,16]{1,0:T(8,128)S(1)} %all_gather.3), channel_id=1, source_target_pairs={{248,0},{0,8},{8,16},{16,24},{24,32},{32,40},{40,48},{48,56},{56,6... | collective-permute-start | bytes 24584 | tf_op jit(solution)/shard_map/ppermute | solution.py:14
  219.3 5.2 %collective-permute-start.3 = (f32[128,16]{1,0:T(8,128)S(1)}, f32[128,16]{1,0:T(8,128)S(1)}, u32[]{:S(2)}, u32[]{:S(2)}) collective-permute-start(f32[128,16]{1,0:T(8,128)S(1)} %all_gather.3), channel_id=1, source_target_pairs={{8,0},{16,8},{24,16},{32,24},{40,32},{48,40},{56,48},{64,56},{72,6... | collective-permute-start | bytes 24584 | tf_op jit(solution)/shard_map/ppermute | solution.py:14
